TPU v7x, 128 devices: a whole 4x4x4 slice. The times are simulated.
128 devices in a mesh: ctx: 32 (over z, x_hi, y), head: 4 (over x_lo, core).
Axes of the slice: x: 4 (x_hi: 2, x_lo: 2; x = x_hi * 2 + x_lo), y: 4, z: 4, core: 2. Of those that a mesh axis runs over, the one named last changes fastest.
Arguments:
- query: bfloat16 [4096, 36864], P('ctx', 'head'), may hold values from -16 to 16
- compressed: bfloat16 [4096, 576], P('ctx'), may hold values from -8 to 8
- segments: int32 [4096], replicated, may hold values from 0 to 2, never falling along the last dimension, each value on 1 to 3072 neighbouring positions
- grad_attn: bfloat16 [4096, 32768], P('ctx', 'head'), may hold values from -6 to 6
Outputs:
- attention: float32 [4096, 32768], P('ctx', 'head')
- grad_query: float32 [4096, 36864], P('ctx', 'head')
- grad_compressed: float32 [4096, 576], P('ctx', 'head')
Inputs may be any that keep to these rules, and one draw needn't show every extreme that they name: `segments`: segment numbers never fall along the trajectory.
All inputs are finite; a program needn't handle non-finite values.
Results may differ from a plain program's by a relative error of at most 0.018.
Values may be sent and summed in bfloat16 or wider, within the bound.
No kernel may reach another device: no remote copies, remote signals or barrier semaphores. Data moves between devices by JAX's collectives and lax.ppermute only.
A program may use at most 128 MiB of HBM per device.

v0:
```python
import math

import jax
import jax.numpy as jnp
from jax import lax
from jax.experimental import pallas as pl
from jax.experimental.pallas import tpu as pltpu
from jax.sharding import PartitionSpec as P

LATENT = 512
ROPE = 64
WIDTH = LATENT + ROPE
ROWS = 128
GROUPS = 16
LANES = ROWS * GROUPS
SEQ = 4096
HALF = WIDTH // 2
PART = WIDTH // 4
KB = 512
MAXB = 7
HEADS = 4
CHUNK = HEADS * ROWS
STEPS = LANES // CHUNK

SCALE = 1.0 / math.sqrt(192.0)
NEG = -1e30

NZ, NXH, NY, NXL, NC = 4, 2, 4, 2, 2
F32, BF16 = jnp.float32, jnp.bfloat16


def flat(z, xh, y, xl, c):
    return ((z * NXH + xh) * NY + y) * (NXL * NC) + xl * NC + c


def send(x, move):
    pairs = []
    for z in range(NZ):
        for xh in range(NXH):
            for y in range(NY):
                for xl in range(NXL):
                    for c in range(NC):
                        to = move(z, xh, y, xl, c)
                        pairs.append((flat(z, xh, y, xl, c), flat(*to)))
    return lax.ppermute(x, ("ctx", "head"), pairs)


def other_core(z, xh, y, xl, c):
    return (z, xh, y, xl, 1 - c)


def across_x(z, xh, y, xl, c):
    return (z, 1 - xh, y, 1 - xl, c)


def along_x(dxh, dxl):
    return lambda z, xh, y, xl, c: (z, (xh + dxh) % NXH, y, (xl + dxl) % NXL, c)


def along(axis, d):
    def move(z, xh, y, xl, c):
        if c == axis:
            return ((z + d) % NZ, xh, y, xl, c)
        return (z, xh, (y + d) % NY, xl, c)

    return move


def collect(own, core, query, grad):
    mine = lax.dynamic_slice_in_dim(own.T, core * HALF, HALF, 0)
    pair = jnp.stack([mine, send(mine, across_x)])
    near = jnp.stack([pair] + [send(pair, along(1, d)) for d in (1, 3, 2)])
    near, query, grad = lax.optimization_barrier((near, query, grad))
    below, above = send(near, along(0, 1)), send(near, along(0, 3))
    below, rows = lax.optimization_barrier((below, lay_out(query, grad)))
    pieces = [near, below, above, send(below, along(0, 1))]
    return pieces + [send(p, other_core) for p in pieces], rows


RING = (0, -1, 1, 2)


def lay_out_kernel(q_ref, g_ref, qt_ref, gt_ref, qn_ref, gn_ref):
    for x_ref, t_ref, n_ref, width in ((q_ref, qt_ref, qn_ref, WIDTH), (g_ref, gt_ref, gn_ref, LATENT)):
        x = x_ref[...]
        turned = x.T
        for h in range(HEADS):
            rows = slice(h * ROWS, (h + 1) * ROWS)
            t_ref[:, rows] = turned[h * width:(h + 1) * width]
            n_ref[rows, :] = x[:, h * width:(h + 1) * width]


def lay_out(query, grad):
    wide = lambda w: pl.BlockSpec((ROWS, HEADS * w), lambda i: (0, i))
    columns = lambda w: pl.BlockSpec((w, CHUNK), lambda i: (0, i))
    rows = lambda w: pl.BlockSpec((CHUNK, w), lambda i: (i, 0))
    shapes = [(WIDTH, LANES), (LATENT, LANES), (LANES, WIDTH), (LANES, LATENT)]
    return pl.pallas_call(
        lay_out_kernel,
        grid=(STEPS,),
        in_specs=[wide(WIDTH), wide(LATENT)],
        out_specs=[columns(WIDTH), columns(LATENT), rows(WIDTH), rows(LATENT)],
        out_shape=[jax.ShapeDtypeStruct(shape, BF16) for shape in shapes],
        compiler_params=pltpu.CompilerParams(
            dimension_semantics=("arbitrary",), vmem_limit_bytes=60 * 1024 * 1024
        ),
        cost_estimate=pl.CostEstimate(flops=0, bytes_accessed=14 * 10**6, transcendentals=0),
        name="lay_out",
    )(query, grad)


def turn_back_kernel(width, x_ref, out_ref):
    x = x_ref[...]
    out_ref[...] = jnp.concatenate(
        [x[:, h * ROWS:(h + 1) * ROWS] for h in range(HEADS)], axis=0
    ).T


def turn_back(x):
    width = x.shape[0]
    return pl.pallas_call(
        lambda *refs: turn_back_kernel(width, *refs),
        grid=(STEPS,),
        in_specs=[pl.BlockSpec((width, CHUNK), lambda i: (0, i))],
        out_specs=pl.BlockSpec((ROWS, HEADS * width), lambda i: (0, i)),
        out_shape=jax.ShapeDtypeStruct((ROWS, GROUPS * width), F32),
        compiler_params=pltpu.CompilerParams(
            dimension_semantics=("arbitrary",), vmem_limit_bytes=60 * 1024 * 1024
        ),
        cost_estimate=pl.CostEstimate(
            flops=0, bytes_accessed=2 * 4 * width * LANES, transcendentals=0
        ),
        name="turn_back",
    )(x)


def attend_kernel(segments, qt0, qt, gt, qn, gn, *rest):
    pieces = rest[:8]
    o_ref, dq_ref, keep_ref = rest[8:11]
    send_refs = rest[11:15]
    (c_v, ct_v, s_v, w_v, acc, top_v, st_f, st_b, zero_f, zero_b, in_sem, out_sem,
     zero_sem, bounds) = rest[15:]
    step = pl.program_id(0)
    ctx, head = lax.axis_index("ctx"), lax.axis_index("head")
    z, xh, y, xl, core = ctx >> 3, (ctx >> 2) & 1, ctx & 3, head >> 1, head & 1

    @pl.when(step == 0)
    def _():
        def halve(_, ends):
            found = []
            for value, (low, high) in zip((1, 2), ends):
                mid = (low + high) >> 1
                less = (low < high) & (segments[jnp.minimum(mid, SEQ - 1)] < value)
                found.append((jnp.where(less, mid + 1, low), jnp.where(less, high, mid)))
            return tuple(found)

        ends = (jnp.int32(0), jnp.int32(SEQ))
        ends = lax.fori_loop(0, 13, halve, (ends, ends))
        bounds[0], bounds[1] = ends[0][0], ends[1][0]

    second, third = bounds[0], bounds[1]

    def start_of(position):
        return jnp.where(position >= third, third, jnp.where(position >= second, second, 0))

    first_row = ctx * ROWS
    first = start_of(first_row) // KB
    blocks = (first_row + ROWS + KB - 1) // KB - first
    free_low, free_high = start_of(first_row + ROWS - 1), first_row + 1
    token = first_row + (lax.broadcasted_iota(jnp.int32, (1, CHUNK), 1) & (ROWS - 1))
    start = start_of(token)

    def off(kb):
        return pl.multiple_of((first + kb) * KB, KB)

    def blk(kb):
        return pl.multiple_of(kb * KB, KB)

    def live(block):
        return (block >= first) & (block < first + blocks)

    def fetch(piece, to, half):
        return pltpu.make_async_copy(
            piece,
            ct_v.at[
                pl.ds(pl.multiple_of(half * HALF, 32), HALF),
                pl.ds(pl.multiple_of((to - first * (KB // ROWS)) * ROWS, ROWS), ROWS),
            ],
            in_sem.at[to, half],
        )

    def fetch_all():
        for n in range(64):
            other, piece, slot, x = n // 32, n // 8 % 4, n // 2 % 4, n % 2
            half = 1 - core if other else core
            dy = jnp.where(half == 0, RING[slot], RING[piece])
            dz = jnp.where(half == 0, RING[piece], RING[slot])
            to = ((z + dz) & 3) * 8 + (xh ^ x) * 4 + ((y + dy) & 3)

            @pl.when(live(to >> 2))
            def _():
                fetch(pieces[other * 4 + piece].at[slot, x], to, half).start()

    def by_core(act):
        for c in range(NC):
            @pl.when(core == c)
            def _():
                act(c)

    def hand_out(block, kept, sent, sems, act):
        dz, x = ((block >> 1) - z) & 3, (block & 1) ^ xh

        def copies(c):
            ref = keep_ref.at[dz, :, x] if c == 0 else keep_ref.at[:, dz, x]
            act(pltpu.make_async_copy(kept(c), ref, sems.at[0]))
            for r, send_ref in enumerate(send_refs):
                if c == 1:
                    @pl.when(dz == r)
                    def _():
                        act(pltpu.make_async_copy(sent(0), send_ref.at[:, x], sems.at[1 + r]))
                else:
                    act(pltpu.make_async_copy(sent(1).at[r], send_ref.at[dz, x], sems.at[1 + r]))

        by_core(copies)

    def clear(block, act):
        @pl.when(jnp.logical_not(live(block)))
        def _():
            hand_out(block, lambda c: zero_f, lambda c: zero_b, zero_sem.at[block], act)

    def deliver_block(kb, act):
        slot = lax.rem(kb, 2)
        hand_out(
            first + kb, lambda c: st_f.at[slot, :, :, c], lambda c: st_b.at[slot, :, :, c],
            out_sem.at[slot], act,
        )

    def begin(copy):
        copy.start()

    def end(copy):
        copy.wait()

    def score(kb, n, masked, q):
        rows = n * KB
        s = jnp.dot(c_v[pl.ds(blk(kb), rows), :], q[...], preferred_element_type=F32)
        if masked:
            key = off(kb) + lax.broadcasted_iota(jnp.int32, (rows, CHUNK), 0)
            s = jnp.where((key >= start) & (key <= token), s, NEG)
        return s

    def folded(x):
        return x.reshape(x.shape[0] // 8, 8, CHUNK)

    def keep_score(kb, n, s, top):
        s_v[pl.ds(blk(kb), n * KB), :] = s
        return jnp.maximum(top, jnp.max(folded(s), axis=0))

    lowest = jnp.full((8, CHUNK), NEG, F32)

    @pl.when(step == 0)
    def _():
        fetch_all()
        zero_f[...] = jnp.zeros_like(zero_f)
        zero_b[...] = jnp.zeros_like(zero_b)
        for block in range(SEQ // KB):
            clear(block, begin)

        def turn(kb, top):
            for t in range(KB // ROWS):
                for half in range(2):
                    fetch(pieces[0].at[0, 0], (first + kb) * (KB // ROWS) + t, half).wait()
            c_v[pl.ds(blk(kb), KB), :] = ct_v[:, pl.ds(blk(kb), KB)].T
            acc[pl.ds(blk(kb), KB), :] = jnp.zeros((KB, WIDTH), F32)
            return keep_score(kb, 1, score(kb, 1, True, qt0), top)

        top_v[...] = lax.fori_loop(0, blocks, turn, lowest)

    top = jnp.max(top_v[...], axis=0, keepdims=True)

    def sweep(body, carried):
        pairs = blocks // 2
        carried = lax.fori_loop(0, pairs, lambda i, c: body(2 * i, 2, c), carried)
        return lax.fori_loop(2 * pairs, blocks, lambda i, c: body(i, 1, c), carried)

    def values(kb, n, total):
        rows = pl.ds(blk(kb), n * KB)
        w_v[rows, :] = jnp.dot(c_v[rows, :LATENT], gt[...], preferred_element_type=F32)
        e = jnp.exp((s_v[rows, :] - top) * SCALE)
        s_v[rows, :] = e
        o_ref[...] += jnp.dot(ct_v[:LATENT, rows], e.astype(BF16), preferred_element_type=F32)
        return total + folded(e).sum(axis=0)

    o_ref[...] = jnp.zeros_like(o_ref)
    total = sweep(values, jnp.zeros((8, CHUNK), F32))
    inverse = 1.0 / jnp.sum(total, axis=0, keepdims=True)
    out = o_ref[...] * inverse
    o_ref[...] = out
    dots = jnp.sum(gt[...].astype(F32) * out, axis=0, keepdims=True)

    dq_ref[...] = jnp.zeros_like(dq_ref)

    def grads(kb, n):
        rows = pl.ds(blk(kb), n * KB)
        p = s_v[rows, :] * inverse
        ds = (p * (w_v[rows, :] - dots) * SCALE).astype(BF16)
        dq_ref[...] += jnp.dot(ct_v[:, rows], ds, preferred_element_type=F32)
        dk = jnp.dot(ds, qn[...], preferred_element_type=F32)
        dv = jnp.dot(p.astype(BF16), gn[...], preferred_element_type=F32)
        acc[rows, :LATENT] += dk[:, :LATENT] + dv
        acc[rows, LATENT:] += dk[:, LATENT:]

    @pl.when(step < STEPS - 1)
    def _():
        def both(kb, n, above):
            def body(masked):
                def run(above):
                    s = score(kb, n, masked, qt)
                    grads(kb, n)
                    return keep_score(kb, n, s, above)

                return run

            free = (off(kb) >= free_low) & (off(kb) + n * KB <= free_high)
            return lax.cond(free, body(False), body(True), above)

        top_v[...] = sweep(both, lowest)

    @pl.when(step == STEPS - 1)
    def _():
        grads(0, 1)

        def stage(kb):
            turned = acc[pl.ds(blk(kb), KB), :].T
            slot = lax.rem(kb, 2)
            for t in range(NY):
                tile = turned[:, t * ROWS:(t + 1) * ROWS].reshape(NXL, NC, PART, ROWS)
                for side in range(NXL):
                    st_f[slot, (t - y) & 3, side ^ xl] = tile[side]
                    st_b[slot, (t - y) & 3, side ^ xl] = tile[side].astype(BF16)

        def room(kb):
            @pl.when(kb >= 2)
            def _():
                deliver_block(kb - 2, end)

        def more(kb, _):
            room(kb - 1)
            stage(kb - 1)
            grads(kb, 1)
            deliver_block(kb - 1, begin)
            return 0

        lax.fori_loop(1, blocks, more, 0)
        room(blocks - 1)
        stage(blocks - 1)
        deliver_block(blocks - 1, begin)

        def finish(kb, _):
            deliver_block(kb, end)
            return 0

        lax.fori_loop(jnp.maximum(blocks - 2, 0), blocks, finish, 0)
        for block in range(SEQ // KB):
            clear(block, end)


def attend(segments, qt, gt, qn, gn, pieces):
    any_spec = pl.BlockSpec(memory_space=pl.ANY)
    tile = (NY, NXL, PART, ROWS)
    staged = (2, NY, NXL, NC, PART, ROWS)
    rings = (NZ, NY, NXH, NXL, PART, ROWS)
    return pl.pallas_call(
        attend_kernel,
        grid_spec=pltpu.PrefetchScalarGridSpec(
            num_scalar_prefetch=1,
            grid=(STEPS,),
            in_specs=[
                pl.BlockSpec((WIDTH, CHUNK), lambda i, s: (0, 0)),
                pl.BlockSpec((WIDTH, CHUNK), lambda i, s: (0, jnp.minimum(i + 1, STEPS - 1))),
                pl.BlockSpec((LATENT, CHUNK), lambda i, s: (0, i)),
                pl.BlockSpec((CHUNK, WIDTH), lambda i, s: (i, 0)),
                pl.BlockSpec((CHUNK, LATENT), lambda i, s: (i, 0)),
            ] + [any_spec] * 8,
            out_specs=[
                pl.BlockSpec((LATENT, CHUNK), lambda i, s: (0, i)),
                pl.BlockSpec((WIDTH, CHUNK), lambda i, s: (0, i)),
            ] + [any_spec] * 5,
            scratch_shapes=[
                pltpu.VMEM((MAXB * KB, WIDTH), BF16),
                pltpu.VMEM((WIDTH, MAXB * KB), BF16),
                pltpu.VMEM((MAXB * KB, CHUNK), F32),
                pltpu.VMEM((MAXB * KB, CHUNK), F32),
                pltpu.VMEM((MAXB * KB, WIDTH), F32),
                pltpu.VMEM((8, CHUNK), F32),
                pltpu.VMEM(staged, F32),
                pltpu.VMEM(staged, BF16),
                pltpu.VMEM(tile, F32),
                pltpu.VMEM(tile, BF16),
                pltpu.SemaphoreType.DMA((SEQ // ROWS, 2)),
                pltpu.SemaphoreType.DMA((2, 5)),
                pltpu.SemaphoreType.DMA((SEQ // KB, 5)),
                pltpu.SMEM((2,), jnp.int32),
            ],
        ),
        out_shape=[
            jax.ShapeDtypeStruct((LATENT, LANES), F32),
            jax.ShapeDtypeStruct((WIDTH, LANES), F32),
            jax.ShapeDtypeStruct(rings, F32),
        ] + [jax.ShapeDtypeStruct(rings[1:], BF16)] * 4,
        compiler_params=pltpu.CompilerParams(
            dimension_semantics=("arbitrary",), vmem_limit_bytes=60 * 1024 * 1024
        ),
        cost_estimate=pl.CostEstimate(
            flops=40 * 10**9, bytes_accessed=30 * 10**6, transcendentals=10**7
        ),
        name="attend",
    )(segments, qt, qt, gt, qn, gn, *pieces)


def deliver(keep, out, attended, query_grad):
    def part(i):
        return keep[i] + send(out[i], other_core).astype(F32)

    def wide(x):
        return x.astype(F32)

    far, attended = lax.optimization_barrier((part(2).astype(BF16), attended))
    far = send(far, along(0, 1))
    attended = turn_back(attended)
    below = part(3).astype(BF16)
    up = (part(1) + wide(far)).astype(BF16)
    up, attended, query_grad = lax.optimization_barrier((up, attended, query_grad))
    up, down = send(up, along(0, 1)), send(below, along(0, 3))
    query_grad = turn_back(query_grad)
    total = part(0) + wide(up) + wide(down)
    parts, query_grad = lax.optimization_barrier((total.astype(BF16), query_grad))
    ring = [wide(send(parts[d], along(1, d))) for d in (1, 3, 2)]
    total = total[0] + ring[0] + ring[1] + ring[2]
    parts = total.astype(BF16)
    ring = [wide(send(parts[a, b], along_x(a, b))) for a, b in ((0, 1), (1, 1), (1, 0))]
    return attended, query_grad, (total[0, 0] + ring[0] + ring[1] + ring[2]).T


def shards(query, compressed, segments, grad_attn):
    pieces, rows = collect(compressed, lax.axis_index("head") % NC, query, grad_attn)
    attended, query_grad, keep, *out = attend(segments, *rows, pieces)
    return deliver(keep, out, attended, query_grad)


def solution(mesh):
    placed = (P("ctx", "head"), P("ctx", None), P(), P("ctx", "head"))
    return jax.shard_map(
        shards,
        mesh=mesh,
        in_specs=placed,
        out_specs=(P("ctx", "head"), P("ctx", "head"), P("ctx", "head")),
        check_vma=False,
    )
```

profile of v0, /device:TPU:0, one launch (start us, length us, event | category | flops | bytes accessed | tf_op | source)
XLA Modules:
  0.0 156.8 jit_solution(10634559295519749954)
XLA Ops:
  0.6 0.9 dynamic-slice_bitcast_fusion
  1.6 2.9 %collective-permute-start = (bf16[288,128]{1,0:T(8,128)(2,1)S(1)}, bf16[288,128]{1,0:T(8,128)(2,1)S(1)}, u32[]{:S(2)}, u32[]{:S(2)}) collective-permute-start(bf16[288,128]{1,0:T(8,128)(2,1)S(1)} %get-tuple-element.70), channel_id=1, source_target_pairs={{0,18},{1,19},{2,16},{3,17},{4,22},{5,23},{6,20},{7,21},{8,26},{9,... | collective-permute-start | bytes 221192 | tf_op jit(solution)/shard_map/ppermute | solution.py:45
  4.5 2.7 %collective-permute-done = bf16[288,128]{1,0:T(8,128)(2,1)S(1)} collective-permute-done((bf16[288,128]{1,0:T(8,128)(2,1)S(1)}, bf16[288,128]{1,0:T(8,128)(2,1)S(1)}, u32[]{:S(2)}, u32[]{:S(2)}) %collective-permute-start) | collective-permute-done | bytes 73760 | tf_op jit(solution)/shard_map/ppermute | solution.py:45
  7.2 3.2 %collective-permute-start.2 = (bf16[2,288,128]{2,1,0:T(8,128)(2,1)S(1)}, bf16[2,288,128]{2,1,0:T(8,128)(2,1)S(1)}, u32[]{:S(2)}, u32[]{:S(2)}) collective-permute-start(bf16[2,288,128]{2,1,0:T(8,128)(2,1)S(1)} %get-tuple-element.68), channel_id=1, source_target_pairs={{0,12},{1,97},{2,14},{3,99},{4,0},{5,101},{6,2},{7,103},{8,4},{9,1... | collective-permute-start | bytes 442376 | tf_op jit(solution)/shard_map/ppermute | solution.py:45
  10.4 2.2 %collective-permute-start.3 = (bf16[2,288,128]{2,1,0:T(8,128)(2,1)S(1)}, bf16[2,288,128]{2,1,0:T(8,128)(2,1)S(1)}, u32[]{:S(2)}, u32[]{:S(2)}) collective-permute-start(bf16[2,288,128]{2,1,0:T(8,128)(2,1)S(1)} %get-tuple-element.68), channel_id=1, source_target_pairs={{0,8},{1,65},{2,10},{3,67},{4,12},{5,69},{6,14},{7,71},{8,0},{9,73... | collective-permute-start | bytes 442376 | tf_op jit(solution)/shard_map/ppermute | solution.py:45
  12.6 0.5 collective-permute-done.2
  13.1 5.3 %collective-permute-done.1 = bf16[2,288,128]{2,1,0:T(8,128)(2,1)S(1)} collective-permute-done((bf16[2,288,128]{2,1,0:T(8,128)(2,1)S(1)}, bf16[2,288,128]{2,1,0:T(8,128)(2,1)S(1)}, u32[]{:S(2)}, u32[]{:S(2)}) %collective-permute-start.1) | collective-permute-done | bytes 147488 | tf_op jit(solution)/shard_map/ppermute | solution.py:45
  18.3 0.0 collective-permute-done.3
  18.3 0.1 pad_maximum_fusion.rest_0_
  18.4 2.2 %collective-permute-start.4 = (bf16[4,2,288,128]{3,2,1,0:T(8,128)(2,1)S(1)}, bf16[4,2,288,128]{3,2,1,0:T(8,128)(2,1)S(1)}, u32[]{:S(2)}, u32[]{:S(2)}) collective-permute-start(bf16[4,2,288,128]{3,2,1,0:T(8,128)(2,1)S(1)} %pad_maximum_fusion.rest_0_), channel_id=1, source_target_pairs={{0,32},{1,5},{2,34},{3,7},{4,36},{5,9},{6,38},{7,11},{8,40},{9,13}... | collective-permute-start | bytes 1769480 | tf_op jit(solution)/shard_map/ppermute | solution.py:45
  20.7 1.9 %collective-permute-start.5 = (bf16[4,2,288,128]{3,2,1,0:T(8,128)(2,1)S(1)}, bf16[4,2,288,128]{3,2,1,0:T(8,128)(2,1)S(1)}, u32[]{:S(2)}, u32[]{:S(2)}) collective-permute-start(bf16[4,2,288,128]{3,2,1,0:T(8,128)(2,1)S(1)} %pad_maximum_fusion.rest_0_), channel_id=1, source_target_pairs={{0,96},{1,13},{2,98},{3,15},{4,100},{5,1},{6,102},{7,3},{8,104},{9... | collective-permute-start | bytes 1769480 | tf_op jit(solution)/shard_map/ppermute | solution.py:45
  22.6 6.6 %lay_out.1 = (bf16[576,2048]{1,0:T(8,128)(2,1)}, bf16[512,2048]{1,0:T(8,128)(2,1)}, bf16[2048,576]{1,0:T(8,128)(2,1)}, bf16[2048,512]{1,0:T(8,128)(2,1)}) custom-call(bf16[128,9216]{1,0:T(8,128)(2,1)} %q_ref, bf16[128,8192]{1,0:T(8,128)(2,1)} %g_ref), custom_call_target="tpu_custom_call" | custom-call | bytes 14000000 | tf_op jit(solution)/shard_map/lay_out/pallas_call | solution.py:98
  29.2 1.2 collective-permute-done.4.rest_1_
  30.4 0.2 collective-permute-start.6
  30.6 0.0 collective-permute-start.7
  30.6 0.5 collective-permute-start.8
  31.1 0.1 collective-permute-start.9
  31.2 10.3 %collective-permute-done.6.rest_3_ = bf16[4,2,288,128]{3,2,1,0:T(8,128)(2,1)S(1)} collective-permute-done((bf16[4,2,288,128]{3,2,1,0:T(8,128)(2,1)S(1)}, bf16[4,2,288,128]{3,2,1,0:T(8,128)(2,1)S(1)}, u32[]{:S(2)}, u32[]{:S(2)}) %collective-permute-start.6) | collective-permute-done | bytes 589856 | tf_op jit(solution)/shard_map/ppermute | solution.py:45
  41.5 2.1 %collective-permute-done.10.rest_7_ = bf16[4,2,288,128]{3,2,1,0:T(8,128)(2,1)} collective-permute-done((bf16[4,2,288,128]{3,2,1,0:T(8,128)(2,1)S(1)}, bf16[4,2,288,128]{3,2,1,0:T(8,128)(2,1)}, u32[]{:S(2)}, u32[]{:S(2)}) %collective-permute-start.10) | collective-permute-done | bytes 589856 | tf_op jit(solution)/shard_map/ppermute | solution.py:45
  43.7 20.2 %attend.1 = (f32[512,2048]{1,0:T(8,128)}, f32[576,2048]{1,0:T(8,128)}, f32[4,4,2,2,144,128]{5,4,3,2,1,0:T(8,128)}, bf16[4,2,2,144,128]{4,3,2,1,0:T(8,128)(2,1)},...) custom-call(s32[4096]{0:T(1024)} %segments.1, ...), custom_call_target="tpu_custom_call" | custom-call | flops 40000000000 | bytes 30000000 | tf_op jit(solution)/shard_map/attend/pallas_call | solution.py:373
  63.8 0.1 collective-permute-start.12
  63.9 0.5 collective-permute-start.16
  64.4 0.1 collective-permute-start.11
  64.5 1.6 %collective-permute-done.12 = bf16[4,2,2,144,128]{4,3,2,1,0:T(8,128)(2,1)S(1)} collective-permute-done((bf16[4,2,2,144,128]{4,3,2,1,0:T(8,128)(2,1)}, bf16[4,2,2,144,128]{4,3,2,1,0:T(8,128)(2,1)S(1)}, u32[]{:S(2)}, u32[]{:S(2)}) %collective-permute-start.12) | collective-permute-done | bytes 589856 | tf_op jit(solution)/shard_map/ppermute | solution.py:45
  66.1 0.8 collective-permute-done.16
  67.0 1.9 %fusion = (bf16[4,2,2,144,128]{4,3,2,1,0:T(8,128)(2,1)S(1)}, bf16[4,2,2,144,128]{4,3,2,1,0:T(8,128)(2,1)S(1)}) fusion(bf16[4,2,2,144,128]{4,3,2,1,0:T(8,128)(2,1)S(1)} %collective-permute-done.16, f32[4,4,2,2,144,128]{5,4,3,2,1,0:T(8,128)} %get-tuple-element.41, bf16[4,2,2,144,128]{4,3,2,1,0:T(8,128)(2,1)S(1)} %collective-permute-done.12), kind=kLoop, calls=%fused_computation.1 | loop fusion | flops 1769472 | bytes 4718592 | tf_op jit(solution)/shard_map/convert_element_type | solution.py:431
  68.9 0.1 collective-permute-start.13
  69.0 0.2 collective-permute-start.14
  69.2 38.0 %collective-permute-start.17 = (bf16[4,2,2,144,128]{4,3,2,1,0:T(8,128)(2,1)S(1)}, bf16[4,2,2,144,128]{4,3,2,1,0:T(8,128)(2,1)S(1)}, u32[]{:S(2)}, u32[]{:S(2)}) collective-permute-start(bf16[4,2,2,144,128]{4,3,2,1,0:T(8,128)(2,1)S(1)} %get-tuple-element.59), channel_id=1, source_target_pairs={{0,96},{1,13},{2,98},{3,15},{4,100},{5,1},{6,102},{7,3},{8,104},{9... | collective-permute-start | bytes 1769480 | tf_op jit(solution)/shard_map/ppermute | solution.py:45
  107.2 5.2 %turn_back.2 = f32[128,8192]{1,0:T(8,128)} custom-call(f32[512,2048]{1,0:T(8,128)} %get-tuple-element.46.refs_0_), custom_call_target="tpu_custom_call" | custom-call | bytes 8388608 | tf_op jit(solution)/shard_map/turn_back/pallas_call | solution.py:121
  112.4 2.2 %collective-permute-done.13 = bf16[4,2,2,144,128]{4,3,2,1,0:T(8,128)(2,1)S(1)} collective-permute-done((bf16[4,2,2,144,128]{4,3,2,1,0:T(8,128)(2,1)S(1)}, bf16[4,2,2,144,128]{4,3,2,1,0:T(8,128)(2,1)S(1)}, u32[]{:S(2)}, u32[]{:S(2)}) %collective-permute-start.13) | collective-permute-done | bytes 589856 | tf_op jit(solution)/shard_map/ppermute | solution.py:45
  114.6 1.5 fusion.5
  116.1 0.1 collective-permute-start.15
  116.2 5.6 %turn_back.3 = f32[128,9216]{1,0:T(8,128)} custom-call(f32[576,2048]{1,0:T(8,128)} %get-tuple-element.52.refs_0_), custom_call_target="tpu_custom_call" | custom-call | bytes 9437184 | tf_op jit(solution)/shard_map/turn_back/pallas_call | solution.py:121
  121.8 5.5 %collective-permute-done.15 = bf16[4,2,2,144,128]{4,3,2,1,0:T(8,128)(2,1)S(1)} collective-permute-done((bf16[4,2,2,144,128]{4,3,2,1,0:T(8,128)(2,1)S(1)}, bf16[4,2,2,144,128]{4,3,2,1,0:T(8,128)(2,1)S(1)}, u32[]{:S(2)}, u32[]{:S(2)}) %collective-permute-start.15) | collective-permute-done | bytes 589856 | tf_op jit(solution)/shard_map/ppermute | solution.py:45
  127.3 1.5 fusion.16
  128.9 0.1 collective-permute-start.18
  128.9 3.4 %collective-permute-start.20 = (bf16[2,2,144,128]{3,2,1,0:T(8,128)(2,1)S(1)}, bf16[2,2,144,128]{3,2,1,0:T(8,128)(2,1)S(1)}, u32[]{:S(2)}, u32[]{:S(2)}) collective-permute-start(bf16[2,2,144,128]{3,2,1,0:T(8,128)(2,1)S(1)} %get-tuple-element.62), channel_id=1, source_target_pairs={{0,8},{1,65},{2,10},{3,67},{4,12},{5,69},{6,14},{7,71},{8,0},{9,73... | collective-permute-start | bytes 442376 | tf_op jit(solution)/shard_map/ppermute | solution.py:45
  132.3 0.1 collective-permute-start.19
  132.5 2.8 %collective-permute-done.18 = bf16[2,2,144,128]{3,2,1,0:T(8,128)(2,1)S(1)} collective-permute-done((bf16[2,2,144,128]{3,2,1,0:T(8,128)(2,1)S(1)}, bf16[2,2,144,128]{3,2,1,0:T(8,128)(2,1)S(1)}, u32[]{:S(2)}, u32[]{:S(2)}) %collective-permute-start.18) | collective-permute-done | bytes 147488 | tf_op jit(solution)/shard_map/ppermute | solution.py:45
  135.3 1.8 %collective-permute-done.20 = bf16[2,2,144,128]{3,2,1,0:T(8,128)(2,1)S(1)} collective-permute-done((bf16[2,2,144,128]{3,2,1,0:T(8,128)(2,1)S(1)}, bf16[2,2,144,128]{3,2,1,0:T(8,128)(2,1)S(1)}, u32[]{:S(2)}, u32[]{:S(2)}) %collective-permute-start.20) | collective-permute-done | bytes 147488 | tf_op jit(solution)/shard_map/ppermute | solution.py:45
  137.0 0.7 collective-permute-done.19
  137.7 0.1 fusion.14
  137.8 0.4 collective-permute-start.21
  138.2 12.8 %collective-permute-start.23 = (bf16[144,128]{1,0:T(8,128)(2,1)S(1)}, bf16[144,128]{1,0:T(8,128)(2,1)S(1)}, u32[]{:S(2)}, u32[]{:S(2)}) collective-permute-start(bf16[144,128]{1,0:T(8,128)(2,1)S(1)} %get-tuple-element.65), channel_id=1, source_target_pairs={{0,16},{1,17},{2,18},{3,19},{4,20},{5,21},{6,22},{7,23},{8,24},{9,... | collective-permute-start | bytes 110600 | tf_op jit(solution)/shard_map/ppermute | solution.py:45
  151.0 2.3 %collective-permute-done.23 = bf16[144,128]{1,0:T(8,128)(2,1)S(1)} collective-permute-done((bf16[144,128]{1,0:T(8,128)(2,1)S(1)}, bf16[144,128]{1,0:T(8,128)(2,1)S(1)}, u32[]{:S(2)}, u32[]{:S(2)}) %collective-permute-start.23) | collective-permute-done | bytes 36896 | tf_op jit(solution)/shard_map/ppermute | solution.py:45
  153.3 2.8 %collective-permute-done.22 = bf16[144,128]{1,0:T(8,128)(2,1)S(1)} collective-permute-done((bf16[144,128]{1,0:T(8,128)(2,1)S(1)}, bf16[144,128]{1,0:T(8,128)(2,1)S(1)}, u32[]{:S(2)}, u32[]{:S(2)}) %collective-permute-start.22) | collective-permute-done | bytes 36896 | tf_op jit(solution)/shard_map/ppermute | solution.py:45
  156.1 0.7 fusion.12
  (28 shorter events, 0.1 us)
Async XLA Ops:
  1.6 5.6 %collective-permute-start = (bf16[288,128]{1,0:T(8,128)(2,1)S(1)}, bf16[288,128]{1,0:T(8,128)(2,1)S(1)}, u32[]{:S(2)}, u32[]{:S(2)}) collective-permute-start(bf16[288,128]{1,0:T(8,128)(2,1)S(1)} %get-tuple-element.70), channel_id=1, source_target_pairs={{0,18},{1,19},{2,16},{3,17},{4,22},{5,23},{6,20},{7,21},{8,26},{9,... | collective-permute-start | bytes 221192 | tf_op jit(solution)/shard_map/ppermute | solution.py:45
  7.2 5.8 %collective-permute-start.2 = (bf16[2,288,128]{2,1,0:T(8,128)(2,1)S(1)}, bf16[2,288,128]{2,1,0:T(8,128)(2,1)S(1)}, u32[]{:S(2)}, u32[]{:S(2)}) collective-permute-start(bf16[2,288,128]{2,1,0:T(8,128)(2,1)S(1)} %get-tuple-element.68), channel_id=1, source_target_pairs={{0,12},{1,97},{2,14},{3,99},{4,0},{5,101},{6,2},{7,103},{8,4},{9,1... | collective-permute-start | bytes 442376 | tf_op jit(solution)/shard_map/ppermute | solution.py:45
  10.4 7.9 %collective-permute-start.1 = (bf16[2,288,128]{2,1,0:T(8,128)(2,1)S(1)}, bf16[2,288,128]{2,1,0:T(8,128)(2,1)S(1)}, u32[]{:S(2)}, u32[]{:S(2)}) collective-permute-start(bf16[2,288,128]{2,1,0:T(8,128)(2,1)S(1)} %get-tuple-element.68), channel_id=1, source_target_pairs={{0,4},{1,33},{2,6},{3,35},{4,8},{5,37},{6,10},{7,39},{8,12},{9,41}... | collective-permute-start | bytes 442376 | tf_op jit(solution)/shard_map/ppermute | solution.py:45
  10.4 7.9 %collective-permute-start.3 = (bf16[2,288,128]{2,1,0:T(8,128)(2,1)S(1)}, bf16[2,288,128]{2,1,0:T(8,128)(2,1)S(1)}, u32[]{:S(2)}, u32[]{:S(2)}) collective-permute-start(bf16[2,288,128]{2,1,0:T(8,128)(2,1)S(1)} %get-tuple-element.68), channel_id=1, source_target_pairs={{0,8},{1,65},{2,10},{3,67},{4,12},{5,69},{6,14},{7,71},{8,0},{9,73... | collective-permute-start | bytes 442376 | tf_op jit(solution)/shard_map/ppermute | solution.py:45
  18.4 12.1 %copy-start = (bf16[4,2,288,128]{3,2,1,0:T(8,128)(2,1)}, bf16[4,2,288,128]{3,2,1,0:T(8,128)(2,1)S(1)}, u32[]{:S(2)}) copy-start(bf16[4,2,288,128]{3,2,1,0:T(8,128)(2,1)S(1)} %pad_maximum_fusion.rest_0_) | copy-start | bytes 1769476
  18.4 12.0 %collective-permute-start.4 = (bf16[4,2,288,128]{3,2,1,0:T(8,128)(2,1)S(1)}, bf16[4,2,288,128]{3,2,1,0:T(8,128)(2,1)S(1)}, u32[]{:S(2)}, u32[]{:S(2)}) collective-permute-start(bf16[4,2,288,128]{3,2,1,0:T(8,128)(2,1)S(1)} %pad_maximum_fusion.rest_0_), channel_id=1, source_target_pairs={{0,32},{1,5},{2,34},{3,7},{4,36},{5,9},{6,38},{7,11},{8,40},{9,13}... | collective-permute-start | bytes 1769480 | tf_op jit(solution)/shard_map/ppermute | solution.py:45
  20.7 10.4 %collective-permute-start.5 = (bf16[4,2,288,128]{3,2,1,0:T(8,128)(2,1)S(1)}, bf16[4,2,288,128]{3,2,1,0:T(8,128)(2,1)S(1)}, u32[]{:S(2)}, u32[]{:S(2)}) collective-permute-start(bf16[4,2,288,128]{3,2,1,0:T(8,128)(2,1)S(1)} %pad_maximum_fusion.rest_0_), channel_id=1, source_target_pairs={{0,96},{1,13},{2,98},{3,15},{4,100},{5,1},{6,102},{7,3},{8,104},{9... | collective-permute-start | bytes 1769480 | tf_op jit(solution)/shard_map/ppermute | solution.py:45
  30.4 13.2 %copy-start.1 = (bf16[4,2,288,128]{3,2,1,0:T(8,128)(2,1)}, bf16[4,2,288,128]{3,2,1,0:T(8,128)(2,1)S(1)}, u32[]{:S(2)}) copy-start(bf16[4,2,288,128]{3,2,1,0:T(8,128)(2,1)S(1)} %collective-permute-done.4.rest_1_) | copy-start | bytes 1769476
  30.4 11.1 %collective-permute-start.6 = (bf16[4,2,288,128]{3,2,1,0:T(8,128)(2,1)S(1)}, bf16[4,2,288,128]{3,2,1,0:T(8,128)(2,1)S(1)}, u32[]{:S(2)}, u32[]{:S(2)}) collective-permute-start(bf16[4,2,288,128]{3,2,1,0:T(8,128)(2,1)S(1)} %collective-permute-done.4.rest_1_), channel_id=1, source_target_pairs={{0,32},{1,5},{2,34},{3,7},{4,36},{5,9},{6,38},{7,11},{8,40},{9,13}... | collective-permute-start | bytes 1769480 | tf_op jit(solution)/shard_map/ppermute | solution.py:45
  30.6 10.9 %collective-permute-start.7 = (bf16[4,2,288,128]{3,2,1,0:T(8,128)(2,1)S(1)}, bf16[4,2,288,128]{3,2,1,0:T(8,128)(2,1)S(1)}, u32[]{:S(2)}, u32[]{:S(2)}) collective-permute-start(bf16[4,2,288,128]{3,2,1,0:T(8,128)(2,1)S(1)} %pad_maximum_fusion.rest_0_), channel_id=1, source_target_pairs={{0,1},{1,0},{2,3},{3,2},{4,5},{5,4},{6,7},{7,6},{8,9},{9,8},{10,11... | collective-permute-start | bytes 1769480 | tf_op jit(solution)/shard_map/ppermute | solution.py:45
  30.6 11.0 %collective-permute-start.8 = (bf16[4,2,288,128]{3,2,1,0:T(8,128)(2,1)S(1)}, bf16[4,2,288,128]{3,2,1,0:T(8,128)(2,1)S(1)}, u32[]{:S(2)}, u32[]{:S(2)}) collective-permute-start(bf16[4,2,288,128]{3,2,1,0:T(8,128)(2,1)S(1)} %collective-permute-done.4.rest_1_), channel_id=1, source_target_pairs={{0,1},{1,0},{2,3},{3,2},{4,5},{5,4},{6,7},{7,6},{8,9},{9,8},{10,11... | collective-permute-start | bytes 1769480 | tf_op jit(solution)/shard_map/ppermute | solution.py:45
  31.1 12.6 %copy-start.2 = (bf16[4,2,288,128]{3,2,1,0:T(8,128)(2,1)}, bf16[4,2,288,128]{3,2,1,0:T(8,128)(2,1)S(1)}, u32[]{:S(2)}) copy-start(bf16[4,2,288,128]{3,2,1,0:T(8,128)(2,1)S(1)} %collective-permute-done.5.rest_2_) | copy-start | bytes 1769476
  31.1 10.4 %collective-permute-start.9 = (bf16[4,2,288,128]{3,2,1,0:T(8,128)(2,1)S(1)}, bf16[4,2,288,128]{3,2,1,0:T(8,128)(2,1)S(1)}, u32[]{:S(2)}, u32[]{:S(2)}) collective-permute-start(bf16[4,2,288,128]{3,2,1,0:T(8,128)(2,1)S(1)} %collective-permute-done.5.rest_2_), channel_id=1, source_target_pairs={{0,1},{1,0},{2,3},{3,2},{4,5},{5,4},{6,7},{7,6},{8,9},{9,8},{10,11... | collective-permute-start | bytes 1769480 | tf_op jit(solution)/shard_map/ppermute | solution.py:45
  41.5 2.1 %copy-start.3 = (bf16[4,2,288,128]{3,2,1,0:T(8,128)(2,1)}, bf16[4,2,288,128]{3,2,1,0:T(8,128)(2,1)S(1)}, u32[]{:S(2)}) copy-start(bf16[4,2,288,128]{3,2,1,0:T(8,128)(2,1)S(1)} %collective-permute-done.6.rest_3_) | copy-start | bytes 1769476
  41.5 2.1 %collective-permute-start.10 = (bf16[4,2,288,128]{3,2,1,0:T(8,128)(2,1)S(1)}, bf16[4,2,288,128]{3,2,1,0:T(8,128)(2,1)}, u32[]{:S(2)}, u32[]{:S(2)}) collective-permute-start(bf16[4,2,288,128]{3,2,1,0:T(8,128)(2,1)S(1)} %collective-permute-done.6.rest_3_), channel_id=1, source_target_pairs={{0,1},{1,0},{2,3},{3,2},{4,5},{5,4},{6,7},{7,6},{8,9},{9,8},{10,11... | collective-permute-start | bytes 1769480 | tf_op jit(solution)/shard_map/ppermute | solution.py:45
  41.5 2.1 %copy-start.4 = (bf16[4,2,288,128]{3,2,1,0:T(8,128)(2,1)}, bf16[4,2,288,128]{3,2,1,0:T(8,128)(2,1)S(1)}, u32[]{:S(2)}) copy-start(bf16[4,2,288,128]{3,2,1,0:T(8,128)(2,1)S(1)} %collective-permute-done.7.rest_4_) | copy-start | bytes 1769476
  41.5 2.1 %copy-start.6 = (bf16[4,2,288,128]{3,2,1,0:T(8,128)(2,1)}, bf16[4,2,288,128]{3,2,1,0:T(8,128)(2,1)S(1)}, u32[]{:S(2)}) copy-start(bf16[4,2,288,128]{3,2,1,0:T(8,128)(2,1)S(1)} %collective-permute-done.9.rest_6_) | copy-start | bytes 1769476
  41.5 2.1 %copy-start.5 = (bf16[4,2,288,128]{3,2,1,0:T(8,128)(2,1)}, bf16[4,2,288,128]{3,2,1,0:T(8,128)(2,1)S(1)}, u32[]{:S(2)}) copy-start(bf16[4,2,288,128]{3,2,1,0:T(8,128)(2,1)S(1)} %collective-permute-done.8.rest_5_) | copy-start | bytes 1769476
  63.8 2.3 %collective-permute-start.12 = (bf16[4,2,2,144,128]{4,3,2,1,0:T(8,128)(2,1)}, bf16[4,2,2,144,128]{4,3,2,1,0:T(8,128)(2,1)S(1)}, u32[]{:S(2)}, u32[]{:S(2)}) collective-permute-start(bf16[4,2,2,144,128]{4,3,2,1,0:T(8,128)(2,1)} %get-tuple-element.43), channel_id=1, source_target_pairs={{0,1},{1,0},{2,3},{3,2},{4,5},{5,4},{6,7},{7,6},{8,9},{9,8},{10,11... | collective-permute-start | bytes 1769480 | tf_op jit(solution)/shard_map/ppermute | solution.py:45
  63.9 3.0 %collective-permute-start.16 = (bf16[4,2,2,144,128]{4,3,2,1,0:T(8,128)(2,1)}, bf16[4,2,2,144,128]{4,3,2,1,0:T(8,128)(2,1)S(1)}, u32[]{:S(2)}, u32[]{:S(2)}) collective-permute-start(bf16[4,2,2,144,128]{4,3,2,1,0:T(8,128)(2,1)} %get-tuple-element.51), channel_id=1, source_target_pairs={{0,1},{1,0},{2,3},{3,2},{4,5},{5,4},{6,7},{7,6},{8,9},{9,8},{10,11... | collective-permute-start | bytes 1769480 | tf_op jit(solution)/shard_map/ppermute | solution.py:45
  64.4 48.0 %collective-permute-start.11 = (bf16[4,2,2,144,128]{4,3,2,1,0:T(8,128)(2,1)}, bf16[4,2,2,144,128]{4,3,2,1,0:T(8,128)(2,1)S(1)}, u32[]{:S(2)}, u32[]{:S(2)}) collective-permute-start(bf16[4,2,2,144,128]{4,3,2,1,0:T(8,128)(2,1)} %get-tuple-element.42), channel_id=1, source_target_pairs={{0,1},{1,0},{2,3},{3,2},{4,5},{5,4},{6,7},{7,6},{8,9},{9,8},{10,11... | collective-permute-start | bytes 1769480 | tf_op jit(solution)/shard_map/ppermute | solution.py:45
  68.9 45.8 %collective-permute-start.13 = (bf16[4,2,2,144,128]{4,3,2,1,0:T(8,128)(2,1)S(1)}, bf16[4,2,2,144,128]{4,3,2,1,0:T(8,128)(2,1)S(1)}, u32[]{:S(2)}, u32[]{:S(2)}) collective-permute-start(bf16[4,2,2,144,128]{4,3,2,1,0:T(8,128)(2,1)S(1)} %get-tuple-element.45), channel_id=1, source_target_pairs={{0,32},{1,5},{2,34},{3,7},{4,36},{5,9},{6,38},{7,11},{8,40},{9,13}... | collective-permute-start | bytes 1769480 | tf_op jit(solution)/shard_map/ppermute | solution.py:45
  69.0 52.8 %collective-permute-start.14 = (bf16[4,2,2,144,128]{4,3,2,1,0:T(8,128)(2,1)}, bf16[4,2,2,144,128]{4,3,2,1,0:T(8,128)(2,1)S(1)}, u32[]{:S(2)}, u32[]{:S(2)}) collective-permute-start(bf16[4,2,2,144,128]{4,3,2,1,0:T(8,128)(2,1)} %get-tuple-element.49), channel_id=1, source_target_pairs={{0,1},{1,0},{2,3},{3,2},{4,5},{5,4},{6,7},{7,6},{8,9},{9,8},{10,11... | collective-permute-start | bytes 1769480 | tf_op jit(solution)/shard_map/ppermute | solution.py:45
  69.2 52.6 %collective-permute-start.17 = (bf16[4,2,2,144,128]{4,3,2,1,0:T(8,128)(2,1)S(1)}, bf16[4,2,2,144,128]{4,3,2,1,0:T(8,128)(2,1)S(1)}, u32[]{:S(2)}, u32[]{:S(2)}) collective-permute-start(bf16[4,2,2,144,128]{4,3,2,1,0:T(8,128)(2,1)S(1)} %get-tuple-element.59), channel_id=1, source_target_pairs={{0,96},{1,13},{2,98},{3,15},{4,100},{5,1},{6,102},{7,3},{8,104},{9... | collective-permute-start | bytes 1769480 | tf_op jit(solution)/shard_map/ppermute | solution.py:45
  116.1 11.2 %collective-permute-start.15 = (bf16[4,2,2,144,128]{4,3,2,1,0:T(8,128)(2,1)S(1)}, bf16[4,2,2,144,128]{4,3,2,1,0:T(8,128)(2,1)S(1)}, u32[]{:S(2)}, u32[]{:S(2)}) collective-permute-start(bf16[4,2,2,144,128]{4,3,2,1,0:T(8,128)(2,1)S(1)} %fusion.5), channel_id=1, source_target_pairs={{0,32},{1,5},{2,34},{3,7},{4,36},{5,9},{6,38},{7,11},{8,40},{9,13}... | collective-permute-start | bytes 1769480 | tf_op jit(solution)/shard_map/ppermute | solution.py:45
  128.9 6.4 %collective-permute-start.18 = (bf16[2,2,144,128]{3,2,1,0:T(8,128)(2,1)S(1)}, bf16[2,2,144,128]{3,2,1,0:T(8,128)(2,1)S(1)}, u32[]{:S(2)}, u32[]{:S(2)}) collective-permute-start(bf16[2,2,144,128]{3,2,1,0:T(8,128)(2,1)S(1)} %get-tuple-element.61), channel_id=1, source_target_pairs={{0,4},{1,33},{2,6},{3,35},{4,8},{5,37},{6,10},{7,39},{8,12},{9,41}... | collective-permute-start | bytes 442376 | tf_op jit(solution)/shard_map/ppermute | solution.py:45
  128.9 8.1 %collective-permute-start.20 = (bf16[2,2,144,128]{3,2,1,0:T(8,128)(2,1)S(1)}, bf16[2,2,144,128]{3,2,1,0:T(8,128)(2,1)S(1)}, u32[]{:S(2)}, u32[]{:S(2)}) collective-permute-start(bf16[2,2,144,128]{3,2,1,0:T(8,128)(2,1)S(1)} %get-tuple-element.62), channel_id=1, source_target_pairs={{0,8},{1,65},{2,10},{3,67},{4,12},{5,69},{6,14},{7,71},{8,0},{9,73... | collective-permute-start | bytes 442376 | tf_op jit(solution)/shard_map/ppermute | solution.py:45
  132.3 5.4 %collective-permute-start.19 = (bf16[2,2,144,128]{3,2,1,0:T(8,128)(2,1)S(1)}, bf16[2,2,144,128]{3,2,1,0:T(8,128)(2,1)S(1)}, u32[]{:S(2)}, u32[]{:S(2)}) collective-permute-start(bf16[2,2,144,128]{3,2,1,0:T(8,128)(2,1)S(1)} %get-tuple-element.63), channel_id=1, source_target_pairs={{0,12},{1,97},{2,14},{3,99},{4,0},{5,101},{6,2},{7,103},{8,4},{9,1... | collective-permute-start | bytes 442376 | tf_op jit(solution)/shard_map/ppermute | solution.py:45
  137.8 13.2 %collective-permute-start.21 = (bf16[144,128]{1,0:T(8,128)(2,1)S(1)}, bf16[144,128]{1,0:T(8,128)(2,1)S(1)}, u32[]{:S(2)}, u32[]{:S(2)}) collective-permute-start(bf16[144,128]{1,0:T(8,128)(2,1)S(1)} %get-tuple-element.64), channel_id=1, source_target_pairs={{0,2},{1,3},{2,0},{3,1},{4,6},{5,7},{6,4},{7,5},{8,10},{9,11},{10,... | collective-permute-start | bytes 110600 | tf_op jit(solution)/shard_map/ppermute | solution.py:45
  138.2 15.1 %collective-permute-start.23 = (bf16[144,128]{1,0:T(8,128)(2,1)S(1)}, bf16[144,128]{1,0:T(8,128)(2,1)S(1)}, u32[]{:S(2)}, u32[]{:S(2)}) collective-permute-start(bf16[144,128]{1,0:T(8,128)(2,1)S(1)} %get-tuple-element.65), channel_id=1, source_target_pairs={{0,16},{1,17},{2,18},{3,19},{4,20},{5,21},{6,22},{7,23},{8,24},{9,... | collective-permute-start | bytes 110600 | tf_op jit(solution)/shard_map/ppermute | solution.py:45
  151.0 5.2 %collective-permute-start.22 = (bf16[144,128]{1,0:T(8,128)(2,1)S(1)}, bf16[144,128]{1,0:T(8,128)(2,1)S(1)}, u32[]{:S(2)}, u32[]{:S(2)}) collective-permute-start(bf16[144,128]{1,0:T(8,128)(2,1)S(1)} %get-tuple-element.66), channel_id=1, source_target_pairs={{0,18},{1,19},{2,16},{3,17},{4,22},{5,23},{6,20},{7,21},{8,26},{9,... | collective-permute-start | bytes 110600 | tf_op jit(solution)/shard_map/ppermute | solution.py:45
where the time goes:
time: 157 us
  starting transfers between devices  69.1 us (44%)
  waiting for transfers between devices  42.7 us (27%)
  Pallas kernels  37.5 us (24%)
  other arithmetic  5.73 us (4%)
    ppermute x24, starting transfers between devices, send(): return lax.ppermute(x, ('ctx', 'head'), pairs)  69.1 us
    ppermute x24, waiting for transfers between devices, send(): return lax.ppermute(x, ('ctx', 'head'), pairs)  42.7 us
    pallas_call x1, Pallas kernels, attend(): pl.pallas_call(attend_kernel, grid_spec=pltpu.PrefetchScalarGridSpec(num_...  20.2 us
    pallas_call x2, Pallas kernels, turn_back(): pl.pallas_call(lambda *refs: turn_back_kernel(width, *refs), grid=(STEPS,...  10.8 us
    pallas_call x1, Pallas kernels, lay_out(): pl.pallas_call(lay_out_kernel, grid=(STEPS,), in_specs=[wide(WIDTH), wide...  6.55 us
  transfers between devices with their start and end apart: 24, of which 15 were waited for; matrix products, arithmetic and copies ran while one was open for 2% of the time, Pallas kernels for 11%

commit v1 on v0

--- a/solution.py
+++ b/solution.py
@@ -279,9 +279,11 @@
     top = jnp.max(top_v[...], axis=0, keepdims=True)
 
     def sweep(body, carried):
-        pairs = blocks // 2
-        carried = lax.fori_loop(0, pairs, lambda i, c: body(2 * i, 2, c), carried)
-        return lax.fori_loop(2 * pairs, blocks, lambda i, c: body(i, 1, c), carried)
+        threes = blocks // 3
+        carried = lax.fori_loop(0, threes, lambda i, c: body(3 * i, 3, c), carried)
+        left = blocks - 3 * threes
+        carried = lax.fori_loop(0, left >> 1, lambda i, c: body(3 * threes, 2, c), carried)
+        return lax.fori_loop(0, left & 1, lambda i, c: body(3 * threes, 1, c), carried)
 
     def values(kb, n, total):
         rows = pl.ds(blk(kb), n * KB)

time: 157 us -> 157 us (level)
  no operation moved by 1% of the time
where the time goes in v1:
time: 157 us
  starting transfers between devices  69 us (44%)
  waiting for transfers between devices  42.7 us (27%)
  Pallas kernels  37.5 us (24%)
  other arithmetic  5.73 us (4%)
    ppermute x24, starting transfers between devices, send(): return lax.ppermute(x, ('ctx', 'head'), pairs)  69 us
    ppermute x24, waiting for transfers between devices, send(): return lax.ppermute(x, ('ctx', 'head'), pairs)  42.7 us
    pallas_call x1, Pallas kernels, attend(): pl.pallas_call(attend_kernel, grid_spec=pltpu.PrefetchScalarGridSpec(num_...  20.2 us
    pallas_call x2, Pallas kernels, turn_back(): pl.pallas_call(lambda *refs: turn_back_kernel(width, *refs), grid=(STEPS,...  10.8 us
    pallas_call x1, Pallas kernels, lay_out(): pl.pallas_call(lay_out_kernel, grid=(STEPS,), in_specs=[wide(WIDTH), wide...  6.55 us
  transfers between devices with their start and end apart: 24, of which 15 were waited for; matrix products, arithmetic and copies ran while one was open for 2% of the time, Pallas kernels for 11%

profile of v1, /device:TPU:0, one launch (start us, length us, event | category | flops | bytes accessed | tf_op | source)
XLA Modules:
  0.0 156.7 jit_solution(3082242398600836354)
XLA Ops:
  0.6 0.9 dynamic-slice_bitcast_fusion
  1.6 2.9 %collective-permute-start = (bf16[288,128]{1,0:T(8,128)(2,1)S(1)}, bf16[288,128]{1,0:T(8,128)(2,1)S(1)}, u32[]{:S(2)}, u32[]{:S(2)}) collective-permute-start(bf16[288,128]{1,0:T(8,128)(2,1)S(1)} %get-tuple-element.70), channel_id=1, source_target_pairs={{0,18},{1,19},{2,16},{3,17},{4,22},{5,23},{6,20},{7,21},{8,26},{9,... | collective-permute-start | bytes 221192 | tf_op jit(solution)/shard_map/ppermute | solution.py:45
  4.5 2.7 %collective-permute-done = bf16[288,128]{1,0:T(8,128)(2,1)S(1)} collective-permute-done((bf16[288,128]{1,0:T(8,128)(2,1)S(1)}, bf16[288,128]{1,0:T(8,128)(2,1)S(1)}, u32[]{:S(2)}, u32[]{:S(2)}) %collective-permute-start) | collective-permute-done | bytes 73760 | tf_op jit(solution)/shard_map/ppermute | solution.py:45
  7.2 3.2 %collective-permute-start.2 = (bf16[2,288,128]{2,1,0:T(8,128)(2,1)S(1)}, bf16[2,288,128]{2,1,0:T(8,128)(2,1)S(1)}, u32[]{:S(2)}, u32[]{:S(2)}) collective-permute-start(bf16[2,288,128]{2,1,0:T(8,128)(2,1)S(1)} %get-tuple-element.68), channel_id=1, source_target_pairs={{0,12},{1,97},{2,14},{3,99},{4,0},{5,101},{6,2},{7,103},{8,4},{9,1... | collective-permute-start | bytes 442376 | tf_op jit(solution)/shard_map/ppermute | solution.py:45
  10.4 2.2 %collective-permute-start.3 = (bf16[2,288,128]{2,1,0:T(8,128)(2,1)S(1)}, bf16[2,288,128]{2,1,0:T(8,128)(2,1)S(1)}, u32[]{:S(2)}, u32[]{:S(2)}) collective-permute-start(bf16[2,288,128]{2,1,0:T(8,128)(2,1)S(1)} %get-tuple-element.68), channel_id=1, source_target_pairs={{0,8},{1,65},{2,10},{3,67},{4,12},{5,69},{6,14},{7,71},{8,0},{9,73... | collective-permute-start | bytes 442376 | tf_op jit(solution)/shard_map/ppermute | solution.py:45
  12.6 0.5 collective-permute-done.2
  13.1 5.3 %collective-permute-done.1 = bf16[2,288,128]{2,1,0:T(8,128)(2,1)S(1)} collective-permute-done((bf16[2,288,128]{2,1,0:T(8,128)(2,1)S(1)}, bf16[2,288,128]{2,1,0:T(8,128)(2,1)S(1)}, u32[]{:S(2)}, u32[]{:S(2)}) %collective-permute-start.1) | collective-permute-done | bytes 147488 | tf_op jit(solution)/shard_map/ppermute | solution.py:45
  18.3 0.0 collective-permute-done.3
  18.3 0.1 pad_maximum_fusion.rest_0_
  18.4 2.2 %collective-permute-start.4 = (bf16[4,2,288,128]{3,2,1,0:T(8,128)(2,1)S(1)}, bf16[4,2,288,128]{3,2,1,0:T(8,128)(2,1)S(1)}, u32[]{:S(2)}, u32[]{:S(2)}) collective-permute-start(bf16[4,2,288,128]{3,2,1,0:T(8,128)(2,1)S(1)} %pad_maximum_fusion.rest_0_), channel_id=1, source_target_pairs={{0,32},{1,5},{2,34},{3,7},{4,36},{5,9},{6,38},{7,11},{8,40},{9,13}... | collective-permute-start | bytes 1769480 | tf_op jit(solution)/shard_map/ppermute | solution.py:45
  20.7 1.9 %collective-permute-start.5 = (bf16[4,2,288,128]{3,2,1,0:T(8,128)(2,1)S(1)}, bf16[4,2,288,128]{3,2,1,0:T(8,128)(2,1)S(1)}, u32[]{:S(2)}, u32[]{:S(2)}) collective-permute-start(bf16[4,2,288,128]{3,2,1,0:T(8,128)(2,1)S(1)} %pad_maximum_fusion.rest_0_), channel_id=1, source_target_pairs={{0,96},{1,13},{2,98},{3,15},{4,100},{5,1},{6,102},{7,3},{8,104},{9... | collective-permute-start | bytes 1769480 | tf_op jit(solution)/shard_map/ppermute | solution.py:45
  22.6 6.6 %lay_out.1 = (bf16[576,2048]{1,0:T(8,128)(2,1)}, bf16[512,2048]{1,0:T(8,128)(2,1)}, bf16[2048,576]{1,0:T(8,128)(2,1)}, bf16[2048,512]{1,0:T(8,128)(2,1)}) custom-call(bf16[128,9216]{1,0:T(8,128)(2,1)} %q_ref, bf16[128,8192]{1,0:T(8,128)(2,1)} %g_ref), custom_call_target="tpu_custom_call" | custom-call | bytes 14000000 | tf_op jit(solution)/shard_map/lay_out/pallas_call | solution.py:98
  29.2 1.2 collective-permute-done.4.rest_1_
  30.4 0.2 collective-permute-start.6
  30.6 0.0 collective-permute-start.7
  30.6 0.5 collective-permute-start.8
  31.1 0.1 collective-permute-start.9
  31.2 10.3 %collective-permute-done.6.rest_3_ = bf16[4,2,288,128]{3,2,1,0:T(8,128)(2,1)S(1)} collective-permute-done((bf16[4,2,288,128]{3,2,1,0:T(8,128)(2,1)S(1)}, bf16[4,2,288,128]{3,2,1,0:T(8,128)(2,1)S(1)}, u32[]{:S(2)}, u32[]{:S(2)}) %collective-permute-start.6) | collective-permute-done | bytes 589856 | tf_op jit(solution)/shard_map/ppermute | solution.py:45
  41.5 2.1 %collective-permute-done.10.rest_7_ = bf16[4,2,288,128]{3,2,1,0:T(8,128)(2,1)} collective-permute-done((bf16[4,2,288,128]{3,2,1,0:T(8,128)(2,1)S(1)}, bf16[4,2,288,128]{3,2,1,0:T(8,128)(2,1)}, u32[]{:S(2)}, u32[]{:S(2)}) %collective-permute-start.10) | collective-permute-done | bytes 589856 | tf_op jit(solution)/shard_map/ppermute | solution.py:45
  43.7 20.2 %attend.1 = (f32[512,2048]{1,0:T(8,128)}, f32[576,2048]{1,0:T(8,128)}, f32[4,4,2,2,144,128]{5,4,3,2,1,0:T(8,128)}, bf16[4,2,2,144,128]{4,3,2,1,0:T(8,128)(2,1)},...) custom-call(s32[4096]{0:T(1024)} %segments.1, ...), custom_call_target="tpu_custom_call" | custom-call | flops 40000000000 | bytes 30000000 | tf_op jit(solution)/shard_map/attend/pallas_call | solution.py:375
  63.9 0.1 collective-permute-start.12
  64.0 0.5 collective-permute-start.16
  64.4 0.1 collective-permute-start.11
  64.5 1.6 %collective-permute-done.12 = bf16[4,2,2,144,128]{4,3,2,1,0:T(8,128)(2,1)S(1)} collective-permute-done((bf16[4,2,2,144,128]{4,3,2,1,0:T(8,128)(2,1)}, bf16[4,2,2,144,128]{4,3,2,1,0:T(8,128)(2,1)S(1)}, u32[]{:S(2)}, u32[]{:S(2)}) %collective-permute-start.12) | collective-permute-done | bytes 589856 | tf_op jit(solution)/shard_map/ppermute | solution.py:45
  66.1 0.8 collective-permute-done.16
  67.0 1.9 %fusion = (bf16[4,2,2,144,128]{4,3,2,1,0:T(8,128)(2,1)S(1)}, bf16[4,2,2,144,128]{4,3,2,1,0:T(8,128)(2,1)S(1)}) fusion(bf16[4,2,2,144,128]{4,3,2,1,0:T(8,128)(2,1)S(1)} %collective-permute-done.16, f32[4,4,2,2,144,128]{5,4,3,2,1,0:T(8,128)} %get-tuple-element.41, bf16[4,2,2,144,128]{4,3,2,1,0:T(8,128)(2,1)S(1)} %collective-permute-done.12), kind=kLoop, calls=%fused_computation.1 | loop fusion | flops 1769472 | bytes 4718592 | tf_op jit(solution)/shard_map/convert_element_type | solution.py:433
  68.9 0.1 collective-permute-start.13
  69.0 0.2 collective-permute-start.14
  69.2 37.6 %collective-permute-start.17 = (bf16[4,2,2,144,128]{4,3,2,1,0:T(8,128)(2,1)S(1)}, bf16[4,2,2,144,128]{4,3,2,1,0:T(8,128)(2,1)S(1)}, u32[]{:S(2)}, u32[]{:S(2)}) collective-permute-start(bf16[4,2,2,144,128]{4,3,2,1,0:T(8,128)(2,1)S(1)} %get-tuple-element.59), channel_id=1, source_target_pairs={{0,96},{1,13},{2,98},{3,15},{4,100},{5,1},{6,102},{7,3},{8,104},{9... | collective-permute-start | bytes 1769480 | tf_op jit(solution)/shard_map/ppermute | solution.py:45
  106.7 5.2 %turn_back.2 = f32[128,8192]{1,0:T(8,128)} custom-call(f32[512,2048]{1,0:T(8,128)} %get-tuple-element.46.refs_0_), custom_call_target="tpu_custom_call" | custom-call | bytes 8388608 | tf_op jit(solution)/shard_map/turn_back/pallas_call | solution.py:121
  112.0 2.2 %collective-permute-done.13 = bf16[4,2,2,144,128]{4,3,2,1,0:T(8,128)(2,1)S(1)} collective-permute-done((bf16[4,2,2,144,128]{4,3,2,1,0:T(8,128)(2,1)S(1)}, bf16[4,2,2,144,128]{4,3,2,1,0:T(8,128)(2,1)S(1)}, u32[]{:S(2)}, u32[]{:S(2)}) %collective-permute-start.13) | collective-permute-done | bytes 589856 | tf_op jit(solution)/shard_map/ppermute | solution.py:45
  114.2 1.5 fusion.5
  115.7 0.1 collective-permute-start.15
  115.7 5.6 %turn_back.3 = f32[128,9216]{1,0:T(8,128)} custom-call(f32[576,2048]{1,0:T(8,128)} %get-tuple-element.52.refs_0_), custom_call_target="tpu_custom_call" | custom-call | bytes 9437184 | tf_op jit(solution)/shard_map/turn_back/pallas_call | solution.py:121
  121.3 5.5 %collective-permute-done.15 = bf16[4,2,2,144,128]{4,3,2,1,0:T(8,128)(2,1)S(1)} collective-permute-done((bf16[4,2,2,144,128]{4,3,2,1,0:T(8,128)(2,1)S(1)}, bf16[4,2,2,144,128]{4,3,2,1,0:T(8,128)(2,1)S(1)}, u32[]{:S(2)}, u32[]{:S(2)}) %collective-permute-start.15) | collective-permute-done | bytes 589856 | tf_op jit(solution)/shard_map/ppermute | solution.py:45
  126.8 1.5 fusion.16
  128.4 0.1 collective-permute-start.18
  128.5 3.4 %collective-permute-start.20 = (bf16[2,2,144,128]{3,2,1,0:T(8,128)(2,1)S(1)}, bf16[2,2,144,128]{3,2,1,0:T(8,128)(2,1)S(1)}, u32[]{:S(2)}, u32[]{:S(2)}) collective-permute-start(bf16[2,2,144,128]{3,2,1,0:T(8,128)(2,1)S(1)} %get-tuple-element.62), channel_id=1, source_target_pairs={{0,8},{1,65},{2,10},{3,67},{4,12},{5,69},{6,14},{7,71},{8,0},{9,73... | collective-permute-start | bytes 442376 | tf_op jit(solution)/shard_map/ppermute | solution.py:45
  131.9 0.1 collective-permute-start.19
  132.0 2.8 %collective-permute-done.18 = bf16[2,2,144,128]{3,2,1,0:T(8,128)(2,1)S(1)} collective-permute-done((bf16[2,2,144,128]{3,2,1,0:T(8,128)(2,1)S(1)}, bf16[2,2,144,128]{3,2,1,0:T(8,128)(2,1)S(1)}, u32[]{:S(2)}, u32[]{:S(2)}) %collective-permute-start.18) | collective-permute-done | bytes 147488 | tf_op jit(solution)/shard_map/ppermute | solution.py:45
  134.8 1.8 %collective-permute-done.20 = bf16[2,2,144,128]{3,2,1,0:T(8,128)(2,1)S(1)} collective-permute-done((bf16[2,2,144,128]{3,2,1,0:T(8,128)(2,1)S(1)}, bf16[2,2,144,128]{3,2,1,0:T(8,128)(2,1)S(1)}, u32[]{:S(2)}, u32[]{:S(2)}) %collective-permute-start.20) | collective-permute-done | bytes 147488 | tf_op jit(solution)/shard_map/ppermute | solution.py:45
  136.6 0.7 collective-permute-done.19
  137.3 0.1 fusion.14
  137.4 0.4 collective-permute-start.21
  137.7 13.2 %collective-permute-start.23 = (bf16[144,128]{1,0:T(8,128)(2,1)S(1)}, bf16[144,128]{1,0:T(8,128)(2,1)S(1)}, u32[]{:S(2)}, u32[]{:S(2)}) collective-permute-start(bf16[144,128]{1,0:T(8,128)(2,1)S(1)} %get-tuple-element.65), channel_id=1, source_target_pairs={{0,16},{1,17},{2,18},{3,19},{4,20},{5,21},{6,22},{7,23},{8,24},{9,... | collective-permute-start | bytes 110600 | tf_op jit(solution)/shard_map/ppermute | solution.py:45
  150.9 2.3 %collective-permute-done.23 = bf16[144,128]{1,0:T(8,128)(2,1)S(1)} collective-permute-done((bf16[144,128]{1,0:T(8,128)(2,1)S(1)}, bf16[144,128]{1,0:T(8,128)(2,1)S(1)}, u32[]{:S(2)}, u32[]{:S(2)}) %collective-permute-start.23) | collective-permute-done | bytes 36896 | tf_op jit(solution)/shard_map/ppermute | solution.py:45
  153.2 2.8 %collective-permute-done.22 = bf16[144,128]{1,0:T(8,128)(2,1)S(1)} collective-permute-done((bf16[144,128]{1,0:T(8,128)(2,1)S(1)}, bf16[144,128]{1,0:T(8,128)(2,1)S(1)}, u32[]{:S(2)}, u32[]{:S(2)}) %collective-permute-start.22) | collective-permute-done | bytes 36896 | tf_op jit(solution)/shard_map/ppermute | solution.py:45
  156.1 0.7 fusion.12
  (28 shorter events, 0.1 us)
Async XLA Ops:
  1.6 5.6 %collective-permute-start = (bf16[288,128]{1,0:T(8,128)(2,1)S(1)}, bf16[288,128]{1,0:T(8,128)(2,1)S(1)}, u32[]{:S(2)}, u32[]{:S(2)}) collective-permute-start(bf16[288,128]{1,0:T(8,128)(2,1)S(1)} %get-tuple-element.70), channel_id=1, source_target_pairs={{0,18},{1,19},{2,16},{3,17},{4,22},{5,23},{6,20},{7,21},{8,26},{9,... | collective-permute-start | bytes 221192 | tf_op jit(solution)/shard_map/ppermute | solution.py:45
  7.2 5.8 %collective-permute-start.2 = (bf16[2,288,128]{2,1,0:T(8,128)(2,1)S(1)}, bf16[2,288,128]{2,1,0:T(8,128)(2,1)S(1)}, u32[]{:S(2)}, u32[]{:S(2)}) collective-permute-start(bf16[2,288,128]{2,1,0:T(8,128)(2,1)S(1)} %get-tuple-element.68), channel_id=1, source_target_pairs={{0,12},{1,97},{2,14},{3,99},{4,0},{5,101},{6,2},{7,103},{8,4},{9,1... | collective-permute-start | bytes 442376 | tf_op jit(solution)/shard_map/ppermute | solution.py:45
  10.4 7.9 %collective-permute-start.1 = (bf16[2,288,128]{2,1,0:T(8,128)(2,1)S(1)}, bf16[2,288,128]{2,1,0:T(8,128)(2,1)S(1)}, u32[]{:S(2)}, u32[]{:S(2)}) collective-permute-start(bf16[2,288,128]{2,1,0:T(8,128)(2,1)S(1)} %get-tuple-element.68), channel_id=1, source_target_pairs={{0,4},{1,33},{2,6},{3,35},{4,8},{5,37},{6,10},{7,39},{8,12},{9,41}... | collective-permute-start | bytes 442376 | tf_op jit(solution)/shard_map/ppermute | solution.py:45
  10.4 7.9 %collective-permute-start.3 = (bf16[2,288,128]{2,1,0:T(8,128)(2,1)S(1)}, bf16[2,288,128]{2,1,0:T(8,128)(2,1)S(1)}, u32[]{:S(2)}, u32[]{:S(2)}) collective-permute-start(bf16[2,288,128]{2,1,0:T(8,128)(2,1)S(1)} %get-tuple-element.68), channel_id=1, source_target_pairs={{0,8},{1,65},{2,10},{3,67},{4,12},{5,69},{6,14},{7,71},{8,0},{9,73... | collective-permute-start | bytes 442376 | tf_op jit(solution)/shard_map/ppermute | solution.py:45
  18.4 12.1 %copy-start = (bf16[4,2,288,128]{3,2,1,0:T(8,128)(2,1)}, bf16[4,2,288,128]{3,2,1,0:T(8,128)(2,1)S(1)}, u32[]{:S(2)}) copy-start(bf16[4,2,288,128]{3,2,1,0:T(8,128)(2,1)S(1)} %pad_maximum_fusion.rest_0_) | copy-start | bytes 1769476
  18.4 12.0 %collective-permute-start.4 = (bf16[4,2,288,128]{3,2,1,0:T(8,128)(2,1)S(1)}, bf16[4,2,288,128]{3,2,1,0:T(8,128)(2,1)S(1)}, u32[]{:S(2)}, u32[]{:S(2)}) collective-permute-start(bf16[4,2,288,128]{3,2,1,0:T(8,128)(2,1)S(1)} %pad_maximum_fusion.rest_0_), channel_id=1, source_target_pairs={{0,32},{1,5},{2,34},{3,7},{4,36},{5,9},{6,38},{7,11},{8,40},{9,13}... | collective-permute-start | bytes 1769480 | tf_op jit(solution)/shard_map/ppermute | solution.py:45
  20.7 10.4 %collective-permute-start.5 = (bf16[4,2,288,128]{3,2,1,0:T(8,128)(2,1)S(1)}, bf16[4,2,288,128]{3,2,1,0:T(8,128)(2,1)S(1)}, u32[]{:S(2)}, u32[]{:S(2)}) collective-permute-start(bf16[4,2,288,128]{3,2,1,0:T(8,128)(2,1)S(1)} %pad_maximum_fusion.rest_0_), channel_id=1, source_target_pairs={{0,96},{1,13},{2,98},{3,15},{4,100},{5,1},{6,102},{7,3},{8,104},{9... | collective-permute-start | bytes 1769480 | tf_op jit(solution)/shard_map/ppermute | solution.py:45
  30.4 13.2 %copy-start.1 = (bf16[4,2,288,128]{3,2,1,0:T(8,128)(2,1)}, bf16[4,2,288,128]{3,2,1,0:T(8,128)(2,1)S(1)}, u32[]{:S(2)}) copy-start(bf16[4,2,288,128]{3,2,1,0:T(8,128)(2,1)S(1)} %collective-permute-done.4.rest_1_) | copy-start | bytes 1769476
  30.4 11.1 %collective-permute-start.6 = (bf16[4,2,288,128]{3,2,1,0:T(8,128)(2,1)S(1)}, bf16[4,2,288,128]{3,2,1,0:T(8,128)(2,1)S(1)}, u32[]{:S(2)}, u32[]{:S(2)}) collective-permute-start(bf16[4,2,288,128]{3,2,1,0:T(8,128)(2,1)S(1)} %collective-permute-done.4.rest_1_), channel_id=1, source_target_pairs={{0,32},{1,5},{2,34},{3,7},{4,36},{5,9},{6,38},{7,11},{8,40},{9,13}... | collective-permute-start | bytes 1769480 | tf_op jit(solution)/shard_map/ppermute | solution.py:45
  30.6 10.9 %collective-permute-start.7 = (bf16[4,2,288,128]{3,2,1,0:T(8,128)(2,1)S(1)}, bf16[4,2,288,128]{3,2,1,0:T(8,128)(2,1)S(1)}, u32[]{:S(2)}, u32[]{:S(2)}) collective-permute-start(bf16[4,2,288,128]{3,2,1,0:T(8,128)(2,1)S(1)} %pad_maximum_fusion.rest_0_), channel_id=1, source_target_pairs={{0,1},{1,0},{2,3},{3,2},{4,5},{5,4},{6,7},{7,6},{8,9},{9,8},{10,11... | collective-permute-start | bytes 1769480 | tf_op jit(solution)/shard_map/ppermute | solution.py:45
  30.6 11.0 %collective-permute-start.8 = (bf16[4,2,288,128]{3,2,1,0:T(8,128)(2,1)S(1)}, bf16[4,2,288,128]{3,2,1,0:T(8,128)(2,1)S(1)}, u32[]{:S(2)}, u32[]{:S(2)}) collective-permute-start(bf16[4,2,288,128]{3,2,1,0:T(8,128)(2,1)S(1)} %collective-permute-done.4.rest_1_), channel_id=1, source_target_pairs={{0,1},{1,0},{2,3},{3,2},{4,5},{5,4},{6,7},{7,6},{8,9},{9,8},{10,11... | collective-permute-start | bytes 1769480 | tf_op jit(solution)/shard_map/ppermute | solution.py:45
  31.1 12.6 %copy-start.2 = (bf16[4,2,288,128]{3,2,1,0:T(8,128)(2,1)}, bf16[4,2,288,128]{3,2,1,0:T(8,128)(2,1)S(1)}, u32[]{:S(2)}) copy-start(bf16[4,2,288,128]{3,2,1,0:T(8,128)(2,1)S(1)} %collective-permute-done.5.rest_2_) | copy-start | bytes 1769476
  31.1 10.4 %collective-permute-start.9 = (bf16[4,2,288,128]{3,2,1,0:T(8,128)(2,1)S(1)}, bf16[4,2,288,128]{3,2,1,0:T(8,128)(2,1)S(1)}, u32[]{:S(2)}, u32[]{:S(2)}) collective-permute-start(bf16[4,2,288,128]{3,2,1,0:T(8,128)(2,1)S(1)} %collective-permute-done.5.rest_2_), channel_id=1, source_target_pairs={{0,1},{1,0},{2,3},{3,2},{4,5},{5,4},{6,7},{7,6},{8,9},{9,8},{10,11... | collective-permute-start | bytes 1769480 | tf_op jit(solution)/shard_map/ppermute | solution.py:45
  41.5 2.1 %copy-start.3 = (bf16[4,2,288,128]{3,2,1,0:T(8,128)(2,1)}, bf16[4,2,288,128]{3,2,1,0:T(8,128)(2,1)S(1)}, u32[]{:S(2)}) copy-start(bf16[4,2,288,128]{3,2,1,0:T(8,128)(2,1)S(1)} %collective-permute-done.6.rest_3_) | copy-start | bytes 1769476
  41.5 2.1 %collective-permute-start.10 = (bf16[4,2,288,128]{3,2,1,0:T(8,128)(2,1)S(1)}, bf16[4,2,288,128]{3,2,1,0:T(8,128)(2,1)}, u32[]{:S(2)}, u32[]{:S(2)}) collective-permute-start(bf16[4,2,288,128]{3,2,1,0:T(8,128)(2,1)S(1)} %collective-permute-done.6.rest_3_), channel_id=1, source_target_pairs={{0,1},{1,0},{2,3},{3,2},{4,5},{5,4},{6,7},{7,6},{8,9},{9,8},{10,11... | collective-permute-start | bytes 1769480 | tf_op jit(solution)/shard_map/ppermute | solution.py:45
  41.5 2.1 %copy-start.4 = (bf16[4,2,288,128]{3,2,1,0:T(8,128)(2,1)}, bf16[4,2,288,128]{3,2,1,0:T(8,128)(2,1)S(1)}, u32[]{:S(2)}) copy-start(bf16[4,2,288,128]{3,2,1,0:T(8,128)(2,1)S(1)} %collective-permute-done.7.rest_4_) | copy-start | bytes 1769476
  41.5 2.1 %copy-start.6 = (bf16[4,2,288,128]{3,2,1,0:T(8,128)(2,1)}, bf16[4,2,288,128]{3,2,1,0:T(8,128)(2,1)S(1)}, u32[]{:S(2)}) copy-start(bf16[4,2,288,128]{3,2,1,0:T(8,128)(2,1)S(1)} %collective-permute-done.9.rest_6_) | copy-start | bytes 1769476
  41.5 2.1 %copy-start.5 = (bf16[4,2,288,128]{3,2,1,0:T(8,128)(2,1)}, bf16[4,2,288,128]{3,2,1,0:T(8,128)(2,1)S(1)}, u32[]{:S(2)}) copy-start(bf16[4,2,288,128]{3,2,1,0:T(8,128)(2,1)S(1)} %collective-permute-done.8.rest_5_) | copy-start | bytes 1769476
  63.9 2.3 %collective-permute-start.12 = (bf16[4,2,2,144,128]{4,3,2,1,0:T(8,128)(2,1)}, bf16[4,2,2,144,128]{4,3,2,1,0:T(8,128)(2,1)S(1)}, u32[]{:S(2)}, u32[]{:S(2)}) collective-permute-start(bf16[4,2,2,144,128]{4,3,2,1,0:T(8,128)(2,1)} %get-tuple-element.43), channel_id=1, source_target_pairs={{0,1},{1,0},{2,3},{3,2},{4,5},{5,4},{6,7},{7,6},{8,9},{9,8},{10,11... | collective-permute-start | bytes 1769480 | tf_op jit(solution)/shard_map/ppermute | solution.py:45
  64.0 3.0 %collective-permute-start.16 = (bf16[4,2,2,144,128]{4,3,2,1,0:T(8,128)(2,1)}, bf16[4,2,2,144,128]{4,3,2,1,0:T(8,128)(2,1)S(1)}, u32[]{:S(2)}, u32[]{:S(2)}) collective-permute-start(bf16[4,2,2,144,128]{4,3,2,1,0:T(8,128)(2,1)} %get-tuple-element.51), channel_id=1, source_target_pairs={{0,1},{1,0},{2,3},{3,2},{4,5},{5,4},{6,7},{7,6},{8,9},{9,8},{10,11... | collective-permute-start | bytes 1769480 | tf_op jit(solution)/shard_map/ppermute | solution.py:45
  64.4 47.5 %collective-permute-start.11 = (bf16[4,2,2,144,128]{4,3,2,1,0:T(8,128)(2,1)}, bf16[4,2,2,144,128]{4,3,2,1,0:T(8,128)(2,1)S(1)}, u32[]{:S(2)}, u32[]{:S(2)}) collective-permute-start(bf16[4,2,2,144,128]{4,3,2,1,0:T(8,128)(2,1)} %get-tuple-element.42), channel_id=1, source_target_pairs={{0,1},{1,0},{2,3},{3,2},{4,5},{5,4},{6,7},{7,6},{8,9},{9,8},{10,11... | collective-permute-start | bytes 1769480 | tf_op jit(solution)/shard_map/ppermute | solution.py:45
  68.9 45.3 %collective-permute-start.13 = (bf16[4,2,2,144,128]{4,3,2,1,0:T(8,128)(2,1)S(1)}, bf16[4,2,2,144,128]{4,3,2,1,0:T(8,128)(2,1)S(1)}, u32[]{:S(2)}, u32[]{:S(2)}) collective-permute-start(bf16[4,2,2,144,128]{4,3,2,1,0:T(8,128)(2,1)S(1)} %get-tuple-element.45), channel_id=1, source_target_pairs={{0,32},{1,5},{2,34},{3,7},{4,36},{5,9},{6,38},{7,11},{8,40},{9,13}... | collective-permute-start | bytes 1769480 | tf_op jit(solution)/shard_map/ppermute | solution.py:45
  69.0 52.3 %collective-permute-start.14 = (bf16[4,2,2,144,128]{4,3,2,1,0:T(8,128)(2,1)}, bf16[4,2,2,144,128]{4,3,2,1,0:T(8,128)(2,1)S(1)}, u32[]{:S(2)}, u32[]{:S(2)}) collective-permute-start(bf16[4,2,2,144,128]{4,3,2,1,0:T(8,128)(2,1)} %get-tuple-element.49), channel_id=1, source_target_pairs={{0,1},{1,0},{2,3},{3,2},{4,5},{5,4},{6,7},{7,6},{8,9},{9,8},{10,11... | collective-permute-start | bytes 1769480 | tf_op jit(solution)/shard_map/ppermute | solution.py:45
  69.2 52.1 %collective-permute-start.17 = (bf16[4,2,2,144,128]{4,3,2,1,0:T(8,128)(2,1)S(1)}, bf16[4,2,2,144,128]{4,3,2,1,0:T(8,128)(2,1)S(1)}, u32[]{:S(2)}, u32[]{:S(2)}) collective-permute-start(bf16[4,2,2,144,128]{4,3,2,1,0:T(8,128)(2,1)S(1)} %get-tuple-element.59), channel_id=1, source_target_pairs={{0,96},{1,13},{2,98},{3,15},{4,100},{5,1},{6,102},{7,3},{8,104},{9... | collective-permute-start | bytes 1769480 | tf_op jit(solution)/shard_map/ppermute | solution.py:45
  115.7 11.2 %collective-permute-start.15 = (bf16[4,2,2,144,128]{4,3,2,1,0:T(8,128)(2,1)S(1)}, bf16[4,2,2,144,128]{4,3,2,1,0:T(8,128)(2,1)S(1)}, u32[]{:S(2)}, u32[]{:S(2)}) collective-permute-start(bf16[4,2,2,144,128]{4,3,2,1,0:T(8,128)(2,1)S(1)} %fusion.5), channel_id=1, source_target_pairs={{0,32},{1,5},{2,34},{3,7},{4,36},{5,9},{6,38},{7,11},{8,40},{9,13}... | collective-permute-start | bytes 1769480 | tf_op jit(solution)/shard_map/ppermute | solution.py:45
  128.4 6.4 %collective-permute-start.18 = (bf16[2,2,144,128]{3,2,1,0:T(8,128)(2,1)S(1)}, bf16[2,2,144,128]{3,2,1,0:T(8,128)(2,1)S(1)}, u32[]{:S(2)}, u32[]{:S(2)}) collective-permute-start(bf16[2,2,144,128]{3,2,1,0:T(8,128)(2,1)S(1)} %get-tuple-element.61), channel_id=1, source_target_pairs={{0,4},{1,33},{2,6},{3,35},{4,8},{5,37},{6,10},{7,39},{8,12},{9,41}... | collective-permute-start | bytes 442376 | tf_op jit(solution)/shard_map/ppermute | solution.py:45
  128.5 8.1 %collective-permute-start.20 = (bf16[2,2,144,128]{3,2,1,0:T(8,128)(2,1)S(1)}, bf16[2,2,144,128]{3,2,1,0:T(8,128)(2,1)S(1)}, u32[]{:S(2)}, u32[]{:S(2)}) collective-permute-start(bf16[2,2,144,128]{3,2,1,0:T(8,128)(2,1)S(1)} %get-tuple-element.62), channel_id=1, source_target_pairs={{0,8},{1,65},{2,10},{3,67},{4,12},{5,69},{6,14},{7,71},{8,0},{9,73... | collective-permute-start | bytes 442376 | tf_op jit(solution)/shard_map/ppermute | solution.py:45
  131.9 5.4 %collective-permute-start.19 = (bf16[2,2,144,128]{3,2,1,0:T(8,128)(2,1)S(1)}, bf16[2,2,144,128]{3,2,1,0:T(8,128)(2,1)S(1)}, u32[]{:S(2)}, u32[]{:S(2)}) collective-permute-start(bf16[2,2,144,128]{3,2,1,0:T(8,128)(2,1)S(1)} %get-tuple-element.63), channel_id=1, source_target_pairs={{0,12},{1,97},{2,14},{3,99},{4,0},{5,101},{6,2},{7,103},{8,4},{9,1... | collective-permute-start | bytes 442376 | tf_op jit(solution)/shard_map/ppermute | solution.py:45
  137.4 13.5 %collective-permute-start.21 = (bf16[144,128]{1,0:T(8,128)(2,1)S(1)}, bf16[144,128]{1,0:T(8,128)(2,1)S(1)}, u32[]{:S(2)}, u32[]{:S(2)}) collective-permute-start(bf16[144,128]{1,0:T(8,128)(2,1)S(1)} %get-tuple-element.64), channel_id=1, source_target_pairs={{0,2},{1,3},{2,0},{3,1},{4,6},{5,7},{6,4},{7,5},{8,10},{9,11},{10,... | collective-permute-start | bytes 110600 | tf_op jit(solution)/shard_map/ppermute | solution.py:45
  137.7 15.5 %collective-permute-start.23 = (bf16[144,128]{1,0:T(8,128)(2,1)S(1)}, bf16[144,128]{1,0:T(8,128)(2,1)S(1)}, u32[]{:S(2)}, u32[]{:S(2)}) collective-permute-start(bf16[144,128]{1,0:T(8,128)(2,1)S(1)} %get-tuple-element.65), channel_id=1, source_target_pairs={{0,16},{1,17},{2,18},{3,19},{4,20},{5,21},{6,22},{7,23},{8,24},{9,... | collective-permute-start | bytes 110600 | tf_op jit(solution)/shard_map/ppermute | solution.py:45
  150.9 5.2 %collective-permute-start.22 = (bf16[144,128]{1,0:T(8,128)(2,1)S(1)}, bf16[144,128]{1,0:T(8,128)(2,1)S(1)}, u32[]{:S(2)}, u32[]{:S(2)}) collective-permute-start(bf16[144,128]{1,0:T(8,128)(2,1)S(1)} %get-tuple-element.66), channel_id=1, source_target_pairs={{0,18},{1,19},{2,16},{3,17},{4,22},{5,23},{6,20},{7,21},{8,26},{9,... | collective-permute-start | bytes 110600 | tf_op jit(solution)/shard_map/ppermute | solution.py:45
